TPU v7x, 32 devices: a whole 2x2x4 slice. The times are simulated.
32 devices in a mesh: dp: 8 (over z, core), expert: 4 (over y, x).
Axes of the slice: x: 2, y: 2, z: 4, core: 2. Of those that a mesh axis runs over, the one named last changes fastest.
Arguments:
- tokens: bfloat16 [4, 1024, 3584], P('expert', 'dp'), may hold values from -6 to 6
- grad_out: bfloat16 [4, 1024, 3584], P('expert', 'dp'), may hold values from -6 to 6
- route_ids: int32 [4, 1024], P('expert', 'dp'), may hold values from 0 to 3, as said below
- route_gates: float32 [4, 1024], P('expert', 'dp'), may hold values from 0.2 to 1
- w_gate: bfloat16 [4, 3584, 1024], P('expert', 'dp'), may hold values from -0.09375 to 0.09375
- w_up: bfloat16 [4, 3584, 1024], P('expert', 'dp'), may hold values from -0.09375 to 0.09375
- w_down: bfloat16 [4, 1024, 3584], P('expert', 'dp'), may hold values from -0.1875 to 0.1875
Outputs:
- moe_out: bfloat16 [4, 1024, 3584], P('expert', 'dp')
- input_grad: bfloat16 [4, 1024, 3584], P('expert', None, 'dp')
- gate_grad: float32 [4, 1024], P('expert', 'dp')
Inputs may be any that keep to these rules, and one draw needn't show every extreme that they name: `route_ids`: among the 128 tokens of one device at most 80 name the same expert; one expert is named by exactly 80 tokens of every device; on one device the counts of the other experts differ by at most one.
All inputs are finite; a program needn't handle non-finite values.
Results may differ from a plain program's by a relative error of at most 0.0057.
Values may be sent and summed in bfloat16 or wider, within the bound.
A program may use at most 128 MiB of HBM per device.

v0:
```python
import jax
import jax.numpy as jnp
from jax import lax
from jax.sharding import PartitionSpec as P


def slot_table(route_line, expert_count, capacity):
    chosen = (route_line[:, None] == jnp.arange(expert_count, dtype=jnp.int32)[None, :]).astype(
        jnp.int32
    )
    placed = jnp.sum((jnp.cumsum(chosen, axis=0) - 1) * chosen, axis=1)
    return route_line * capacity + placed


def local(tokens, grad_out, route_ids, route_gates, w_gate, w_up, w_down):
    expert_count = lax.axis_size("expert")
    tok_count = tokens.shape[1]
    width = tokens.shape[2]
    capacity = max(2, 5 * tok_count // (2 * expert_count))
    own_ids = route_ids[0]
    own_slots = slot_table(own_ids, expert_count, capacity)
    slot_owner = jnp.full((expert_count * capacity,), tok_count, jnp.int32)
    slot_owner = slot_owner.at[own_slots].set(jnp.arange(tok_count, dtype=jnp.int32))
    own_tokens = tokens[0]
    own_grad = grad_out[0]
    gate_column = route_gates[0][:, None]
    scaled_grad = (gate_column * own_grad.astype(jnp.float32)).astype(jnp.bfloat16)
    zero_row = jnp.zeros((1, width), jnp.bfloat16)
    send_tokens = jnp.concatenate([own_tokens, zero_row])[slot_owner].reshape(
        expert_count, capacity, width
    )
    send_grad = jnp.concatenate([scaled_grad, zero_row])[slot_owner].reshape(
        expert_count, capacity, width
    )
    arrived_tokens = lax.all_to_all(send_tokens, "expert", split_axis=0, concat_axis=0, tiled=True)
    routed = arrived_tokens.reshape(expert_count * capacity, width)
    full_gate, full_up, full_down = (
        lax.all_gather(w_gate, "dp", axis=1, tiled=True),
        lax.all_gather(w_up, "dp", axis=1, tiled=True),
        lax.all_gather(w_down, "dp", axis=1, tiled=True),
    )
    gate_matrix = full_gate[0]
    up_matrix = full_up[0]
    down_matrix = full_down[0]
    gate_pre = jnp.dot(routed, gate_matrix, preferred_element_type=jnp.float32)
    up_pre = jnp.dot(routed, up_matrix, preferred_element_type=jnp.float32)
    sigmoid_gate = jax.nn.sigmoid(gate_pre)
    silu_gate = gate_pre * sigmoid_gate
    hidden = (silu_gate * up_pre).astype(jnp.bfloat16)
    expert_out = jnp.dot(hidden, down_matrix, preferred_element_type=jnp.float32).astype(
        jnp.bfloat16
    )
    returned = lax.all_to_all(
        expert_out.reshape(expert_count, capacity, width),
        "expert",
        split_axis=0,
        concat_axis=0,
        tiled=True,
    )
    token_out = returned.reshape(expert_count * capacity, width)[own_slots]
    moe_out = (gate_column * token_out.astype(jnp.float32)).astype(jnp.bfloat16)
    gate_grad = jnp.sum(own_grad.astype(jnp.float32) * token_out.astype(jnp.float32), axis=1)
    arrived_grad = lax.all_to_all(send_grad, "expert", split_axis=0, concat_axis=0, tiled=True)
    routed_grad = arrived_grad.reshape(expert_count * capacity, width)
    hidden_grad = jnp.dot(routed_grad, down_matrix.T, preferred_element_type=jnp.float32)
    gate_pre_grad = (
        hidden_grad * up_pre * sigmoid_gate * (1.0 + gate_pre * (1.0 - sigmoid_gate))
    ).astype(jnp.bfloat16)
    up_pre_grad = (hidden_grad * silu_gate).astype(jnp.bfloat16)
    total = jnp.dot(gate_pre_grad, gate_matrix.T, preferred_element_type=jnp.float32)
    input_rows = (
        total + jnp.dot(up_pre_grad, up_matrix.T, preferred_element_type=jnp.float32)
    ).astype(jnp.bfloat16)
    home_rows = lax.all_to_all(
        input_rows.reshape(expert_count, capacity, width),
        "expert",
        split_axis=0,
        concat_axis=0,
        tiled=True,
    )
    token_grad = home_rows.reshape(expert_count * capacity, width)[own_slots]
    input_grad = lax.all_to_all(token_grad[None], "dp", split_axis=2, concat_axis=1, tiled=True)
    return (moe_out[None], input_grad, gate_grad[None])


def solution(mesh):
    in_specs = (
        P("expert", "dp", None),
        P("expert", "dp", None),
        P("expert", "dp"),
        P("expert", "dp"),
        P("expert", "dp", None),
        P("expert", "dp", None),
        P("expert", "dp", None),
    )
    out_specs = (P("expert", "dp", None), P("expert", None, "dp"), P("expert", "dp"))
    return jax.shard_map(local, mesh=mesh, in_specs=in_specs, out_specs=out_specs, check_vma=False)
```

profile of v0, /device:TPU:0, one launch (start us, length us, event | category | flops | bytes accessed | tf_op | source)
XLA Modules:
  0.0 416.3 jit_solution(1568874448295475949)
XLA Ops:
  7.2 0.0 all-gather.4.cloned.1.call-start
  7.2 0.7 all-gather.4.cloned.1.call-update
  7.9 0.0 all-gather.6.cloned.1.call-start
  8.0 0.7 all-gather.6.cloned.1.call-update
  8.7 0.0 all-gather.8.cloned.1.call-start
  8.7 0.7 all-gather.8.cloned.1.call-update
  9.4 0.0 copy-done.4
  9.4 0.1 fusion.29
  9.5 0.2 reduce_window_sum.11
  9.7 0.1 concatenate.6
  9.7 0.2 select_reduce_fusion
  9.9 1.0 scatter_custom_fusion
  11.0 3.1 gather_fusion
  14.1 32.7 %all_to_all.38 = bf16[4,80,3584]{2,1,0:T(8,128)(2,1)} all-to-all(bf16[4,80,3584]{2,1,0:T(8,128)(2,1)S(1)} %bitcast.67), channel_id=1, replica_groups=mesh['dp'=8,'expert'=4] {'expert'}, dimensions={0} | all-to-all | bytes 4587520 | tf_op jit(solution)/shard_map/all_to_all | solution.py:35
  46.8 39.0 %all-gather.4.cloned.1.call-done = bf16[1,3584,1024]{2,1,0:T(8,128)(2,1)} async-done(((bf16[1,448,1024]{2,1,0:T(8,128)(2,1)}), bf16[1,3584,1024]{2,1,0:T(8,128)(2,1)}) %all-gather.4.cloned.1.call-update) | async-done | bytes 7340048 | tf_op jit(solution)/shard_map/all_gather | solution.py:38
  85.8 7.5 %fusion.10 = f32[320,1024]{1,0:T(8,128)} fusion(bf16[320,3584]{1,0:T(8,128)(2,1)} %bitcast.72, bf16[1,3584,1024]{2,1,0:T(8,128)(2,1)} %all-gather.4.cloned.1.call-done), kind=kOutput, calls=%fused_computation.15 | convolution fusion | flops 2348810240 | bytes 10944512 | tf_op jit(solution)/shard_map/dot_general | solution.py:45
  93.3 66.2 %all-gather.6.cloned.1.call-done = bf16[1,3584,1024]{2,1,0:T(8,128)(2,1)} async-done(((bf16[1,448,1024]{2,1,0:T(8,128)(2,1)}), bf16[1,3584,1024]{2,1,0:T(8,128)(2,1)}) %all-gather.6.cloned.1.call-update) | async-done | bytes 7340048 | tf_op jit(solution)/shard_map/all_gather | solution.py:39
  159.5 6.8 %fusion.6 = f32[320,1024]{1,0:T(8,128)} fusion(bf16[320,3584]{1,0:T(8,128)(2,1)S(1)} %bitcast.73, bf16[1,3584,1024]{2,1,0:T(8,128)(2,1)} %all-gather.6.cloned.1.call-done), kind=kOutput, calls=%fused_computation.11 | convolution fusion | flops 2348810240 | bytes 10944512 | tf_op jit(solution)/shard_map/dot_general | solution.py:46
  166.2 66.9 %all-gather.8.cloned.1.call-done = bf16[1,1024,3584]{2,1,0:T(8,128)(2,1)} async-done(((bf16[1,128,3584]{2,1,0:T(8,128)(2,1)}), bf16[1,1024,3584]{2,1,0:T(8,128)(2,1)}) %all-gather.8.cloned.1.call-update) | async-done | bytes 7340048 | tf_op jit(solution)/shard_map/all_gather | solution.py:40
  233.1 7.9 %fusion.18 = bf16[320,3584]{1,0:T(8,128)(2,1)} fusion(bf16[1,1024,3584]{2,1,0:T(8,128)(2,1)} %all-gather.8.cloned.1.call-done, f32[320,1024]{1,0:T(8,128)} %fusion.6, f32[320,1024]{1,0:T(8,128)} %fusion.10), kind=kOutput, calls=%fused_computation.19 | convolution fusion | flops 2351923200 | bytes 12255232 | tf_op jit(solution)/shard_map/dot_general | solution.py:50
  241.0 3.7 all-to-all-start.1
  244.7 27.6 %all-to-all-done.1 = bf16[4,80,3584]{2,1,0:T(8,128)(2,1)S(1)} async-done(((bf16[4,80,3584]{2,1,0:T(8,128)(2,1)}), bf16[4,80,3584]{2,1,0:T(8,128)(2,1)S(1)}, u32[]{:S(2)}, u32[]{:S(2)}) %all-to-all-start.1) | async-done | bytes 2293792 | tf_op jit(solution)/shard_map/all_to_all | solution.py:53
  272.3 1.1 gather_fusion.1
  273.4 0.0 copy-start
  273.4 2.5 fusion.24
  275.9 0.1 concatenate.7
  276.0 3.1 gather_fusion.2
  279.1 0.0 slice-start.2
  279.1 30.1 %all_to_all.39 = bf16[4,80,3584]{2,1,0:T(8,128)(2,1)S(1)} all-to-all(bf16[4,80,3584]{2,1,0:T(8,128)(2,1)S(1)} %bitcast.66), channel_id=1, replica_groups=mesh['dp'=8,'expert'=4] {'expert'}, dimensions={0} | all-to-all | bytes 4587520 | tf_op jit(solution)/shard_map/all_to_all | solution.py:63
  309.3 5.8 %fusion = f32[320,1024]{1,0:T(8,128)S(1)} fusion(bf16[320,3584]{1,0:T(8,128)(2,1)S(1)} %bitcast.76, bf16[1,1024,3584]{2,1,0:T(8,128)(2,1)} %all-gather.8.cloned.1.call-done), kind=kOutput, calls=%fused_computation.5 | convolution fusion | flops 2348810240 | bytes 10944512 | tf_op jit(solution)/shard_map/dot_general | solution.py:65
  315.1 1.1 copy-done.7
  316.2 0.0 slice-done.3
  316.2 0.0 slice-start.1
  316.2 4.8 %fusion.4 = f32[320,3584]{1,0:T(8,128)} fusion(bf16[1,3584,1024]{2,1,0:T(8,128)(2,1)S(1)} %bitcast.87, f32[320,1024]{1,0:T(8,128)S(1)} %fusion, f32[320,1024]{1,0:T(8,128)S(1)} %copy-done.6), kind=kOutput, calls=%fused_computation.9 | convolution fusion | flops 2350776320 | bytes 14548992 | tf_op jit(solution)/shard_map/dot_general | solution.py:72
  320.9 6.0 %fusion.15 = bf16[320,3584]{1,0:T(8,128)(2,1)S(1)} fusion(f32[320,3584]{1,0:T(8,128)} %fusion.4, bf16[1,3584,1024]{2,1,0:T(8,128)(2,1)S(1)} %bitcast.85, f32[320,1024]{1,0:T(8,128)S(1)} %copy-done.6, f32[320,1024]{1,0:T(8,128)} %copy-done.7, f32[320,1024]{1,0:T(8,128)} %fusion.6), kind=kOutput, calls=%fused_computation.18 | convolution fusion | flops 2354380800 | bytes 18153472 | tf_op jit(solution)/shard_map/dot_general | solution.py:70
  326.9 28.4 %all_to_all.40 = bf16[4,80,3584]{2,1,0:T(8,128)(2,1)S(1)} all-to-all(bf16[4,80,3584]{2,1,0:T(8,128)(2,1)S(1)} %bitcast.75), channel_id=1, replica_groups=mesh['dp'=8,'expert'=4] {'expert'}, dimensions={0} | all-to-all | bytes 4587520 | tf_op jit(solution)/shard_map/all_to_all | solution.py:74
  355.3 1.1 gather_fusion.3
  356.5 2.5 copy.14
  359.0 0.5 broadcast.103
  359.5 19.7 %reduce = bf16[3584,128]{1,0:T(8,128)(2,1)S(1)} reduce(bf16[3584,1,128]{2,1,0:T(2,128)(2,1)S(1)} %bitcast.68, bf16[]{:T(256)} %broadcast.103), dimensions={1}, to_apply=%bitcast.58.reduce_sub_computation | reduce | bytes 1835010
  379.2 0.0 copy-start.1
  379.2 1.1 reshape.155
  380.3 3.6 all-to-all-start.4
  383.9 1.1 fusion.22
  385.0 22.6 %all-to-all-done.4 = bf16[8,2,28672]{2,1,0:T(2,128)(2,1)S(1)} async-done(((bf16[8,2,28672]{2,1,0:T(2,128)(2,1)}), bf16[8,2,28672]{2,1,0:T(2,128)(2,1)S(1)}, u32[]{:S(2)}, u32[]{:S(2)}) %all-to-all-start.4) | async-done | bytes 917536 | tf_op jit(solution)/shard_map/all_to_all | solution.py:82
  407.6 0.9 reshape.156
  408.5 0.1 copy.16
  408.6 1.2 copy.19
  (24 shorter events, 0.1 us)
Async XLA Ops:
  7.2 2.2 copy-start.4
  7.2 2.5 copy-start.3
  7.2 78.6 %all-gather.4.cloned.1.call-start = ((), (), s32[]{:S(2)}) async-start(), calls=%async_computation.5 | async-start | bytes 8257536 | tf_op jit(solution)/shard_map/all_gather | solution.py:38
  7.9 151.5 %all-gather.6.cloned.1.call-start = ((), (), s32[]{:S(2)}) async-start(), calls=%async_computation.6 | async-start | bytes 8257536 | tf_op jit(solution)/shard_map/all_gather | solution.py:39
  8.7 224.5 %all-gather.8.cloned.1.call-start = ((), (), s32[]{:S(2)}) async-start(), calls=%async_computation.7 | async-start | bytes 8257536 | tf_op jit(solution)/shard_map/all_gather | solution.py:40
  85.8 73.7 %copy-start.2 = (bf16[4,80,3584]{2,1,0:T(8,128)(2,1)S(1)}, bf16[4,80,3584]{2,1,0:T(8,128)(2,1)}, u32[]{:S(2)}) copy-start(bf16[4,80,3584]{2,1,0:T(8,128)(2,1)} %all_to_all.38) | copy-start | bytes 6881284
  241.0 31.3 %all-to-all-start.1 = ((bf16[4,80,3584]{2,1,0:T(8,128)(2,1)}), bf16[4,80,3584]{2,1,0:T(8,128)(2,1)S(1)}, u32[]{:S(2)}, u32[]{:S(2)}) async-start(bf16[4,80,3584]{2,1,0:T(8,128)(2,1)} %bitcast.74), calls=%async_computation.1 | async-start | bytes 4587520 | tf_op jit(solution)/shard_map/all_to_all | solution.py:53
  272.3 1.1 copy-start.5
  273.4 2.5 copy-start
  279.1 37.1 %slice-start.2 = ((s8[7340032]{0:T(1024)(128)(4,1)}), s8[4194304]{0:T(1024)(128)(4,1)S(1)}, s32[]{:S(2)}) async-start(s8[7340032]{0:T(1024)(128)(4,1)} %bitcast.86), calls=%async_computation.10 | async-start | bytes 8388608
  309.3 6.9 %slice-start.3 = ((s8[7340032]{0:T(1024)(128)(4,1)}), s8[3145728]{0:T(1024)(128)(4,1)S(1)}, s32[]{:S(2)}) async-start(s8[7340032]{0:T(1024)(128)(4,1)} %bitcast.86), calls=%async_computation.11 | async-start | bytes 6291456
  309.3 6.9 %copy-start.6 = (f32[320,1024]{1,0:T(8,128)S(1)}, f32[320,1024]{1,0:T(8,128)}, u32[]{:S(2)}) copy-start(f32[320,1024]{1,0:T(8,128)} %fusion.10) | copy-start | bytes 3932164
  309.3 11.7 %slice-start = ((s8[7340032]{0:T(1024)(128)(4,1)}), s8[4194304]{0:T(1024)(128)(4,1)S(1)}, s32[]{:S(2)}) async-start(s8[7340032]{0:T(1024)(128)(4,1)} %bitcast.84), calls=%async_computation.8 | async-start | bytes 8388608
  315.1 1.1 copy-start.7
  316.2 4.8 %slice-start.1 = ((s8[7340032]{0:T(1024)(128)(4,1)}), s8[3145728]{0:T(1024)(128)(4,1)S(1)}, s32[]{:S(2)}) async-start(s8[7340032]{0:T(1024)(128)(4,1)} %bitcast.84), calls=%async_computation.9 | async-start | bytes 6291456
  379.2 4.7 %copy-start.1 = (bf16[128,3584]{1,0:T(8,128)(2,1)S(1)}, bf16[128,3584]{1,0:T(8,128)(2,1)}, u32[]{:S(2)}) copy-start(bf16[128,3584]{1,0:T(8,128)(2,1)} %copy-done) | copy-start | bytes 2752516
  380.3 27.3 %all-to-all-start.4 = ((bf16[8,2,28672]{2,1,0:T(2,128)(2,1)}), bf16[8,2,28672]{2,1,0:T(2,128)(2,1)S(1)}, u32[]{:S(2)}, u32[]{:S(2)}) async-start(bf16[8,2,28672]{2,1,0:T(2,128)(2,1)} %reshape.155), calls=%async_computation.4 | async-start | bytes 1835008 | tf_op jit(solution)/shard_map/all_to_all | solution.py:82
Sparse Core Ops, SparseCore 0:
  9.7 76.0 all-gather.3
  87.4 71.9 all-gather.5
  161.1 71.9 all-gather.7
where the time goes:
time: 417 us; the launch traced here: 416 us
  waiting for transfers between devices  224 us (54%)
  blocking collectives  91.3 us (22%)
  matrix products  38.7 us (9%)
  other arithmetic  23.7 us (6%)
  local copies, waits for them, and re-layouts  17.1 us (4%)
  between operations  14 us (3%)
  starting transfers between devices  7.35 us (2%)
    all_gather x1, waiting for transfers between devices, local(): lax.all_gather(w_down, 'dp', axis=1, tiled=True)  66.9 us
    all_gather x1, waiting for transfers between devices, local(): lax.all_gather(w_up, 'dp', axis=1, tiled=True)  66.2 us
    all_gather x1, waiting for transfers between devices, local(): lax.all_gather(w_gate, 'dp', axis=1, tiled=True)  39 us
    all_to_all x1, blocking collectives, local(): lax.all_to_all(send_tokens, 'expert', split_axis=0, concat_axis=0, tiled=...  32.7 us
    all_to_all x1, blocking collectives, local(): lax.all_to_all(send_grad, 'expert', split_axis=0, concat_axis=0, tiled=True)  30.1 us
    all_to_all x1, blocking collectives, local(): lax.all_to_all(input_rows.reshape(expert_count, capacity, width), 'expert...  28.4 us
    all_to_all x1, waiting for transfers between devices, local(): lax.all_to_all(expert_out.reshape(expert_count, capacity, width), 'expert...  27.6 us
    all_to_all x1, waiting for transfers between devices, local(): lax.all_to_all(token_grad[None], 'dp', split_axis=2, concat_axis=1, tiled...  22.6 us
  transfers between devices with their start and end apart: 5, of which 5 were waited for; matrix products, arithmetic and copies ran while one was open for 5% of the time, Pallas kernels for 0%

commit v1 on v0

--- a/solution.py
+++ b/solution.py
@@ -2,6 +2,19 @@
 import jax.numpy as jnp
 from jax import lax
 from jax.sharding import PartitionSpec as P
+
+
+def ring_gather(shard, axis, dim):
+    ways = lax.axis_size(axis)
+    up = [(d, (d + 1) % ways) for d in range(ways)]
+    down = [(d, (d - 1) % ways) for d in range(ways)]
+    earlier, later = ([shard], [shard])
+    for _ in range(ways // 2):
+        earlier.append(lax.ppermute(earlier[-1], axis, up))
+    for _ in range((ways - 1) // 2):
+        later.append(lax.ppermute(later[-1], axis, down))
+    line = jnp.concatenate([*earlier[::-1], *later[1:]], axis=dim)
+    return jnp.roll(line, (lax.axis_index(axis) - ways // 2) * shard.shape[dim], axis=dim)
 
 
 def slot_table(route_line, expert_count, capacity):
@@ -37,7 +50,7 @@
     full_gate, full_up, full_down = (
         lax.all_gather(w_gate, "dp", axis=1, tiled=True),
         lax.all_gather(w_up, "dp", axis=1, tiled=True),
-        lax.all_gather(w_down, "dp", axis=1, tiled=True),
+        ring_gather(w_down, "dp", 1),
     )
     gate_matrix = full_gate[0]
     up_matrix = full_up[0]

time: 417 us -> 400 us (0.959)
  blocking collectives: 91.3 us -> 58.6 us
  waiting for transfers between devices: 224 us -> 194 us
  local copies, waits for them, and re-layouts: 17.1 us -> 42 us
  starting transfers between devices: 7.35 us -> 29.5 us
    ppermute x0 -> x7, waiting for transfers between devices: none -> 99.2 us  [the longest x4 98.1 us: ring_gather(): earlier.append(lax.ppermute(earlier[-1], axis, up))]
    all_gather x1 -> x0, waiting for transfers between devices: 66.9 us -> none  [local(): lax.all_gather(w_down, 'dp', axis=1, tiled=True)]
    all_gather x1, waiting for transfers between devices: 39 us -> 0.01 us  [local(): lax.all_gather(w_gate, 'dp', axis=1, tiled=True)]
    all_to_all x1 -> x0, blocking collectives: 32.7 us -> none  [local(): lax.all_to_all(send_tokens, 'expert', split_axis=0, concat_axis=0, tiled=...]
    all_gather x1, waiting for transfers between devices: 66.2 us -> 43.1 us  [local(): lax.all_gather(w_up, 'dp', axis=1, tiled=True)]
    unnamed x28 -> x49, local copies, waits for them, and re-layouts: 3.81 us -> 26 us
    ppermute x0 -> x7, starting transfers between devices: none -> 13.8 us  [the longest x3 7.01 us: ring_gather(): later.append(lax.ppermute(later[-1], axis, down))]
    all_to_all x0 -> x1, starting transfers between devices: none -> 4.59 us  [local(): lax.all_to_all(send_tokens, 'expert', split_axis=0, concat_axis=0, tiled=...]
  transfers between devices with their start and end apart: 5 -> 12, of which waited for: 5 -> 8; matrix products, arithmetic and copies ran while one was open for 5% -> 9% of each run, Pallas kernels for 0% -> 0%
where the time goes in v1:
time: 400 us; the launch traced here: 399 us
  waiting for transfers between devices  194 us (48%)
  blocking collectives  58.6 us (15%)
  local copies, waits for them, and re-layouts  42 us (10%)
  matrix products  36.6 us (9%)
  starting transfers between devices  29.5 us (7%)
  other arithmetic  24.4 us (6%)
  between operations  14.4 us (4%)
    ppermute x4, waiting for transfers between devices, ring_gather(): earlier.append(lax.ppermute(earlier[-1], axis, up))  98.1 us
    all_gather x1, waiting for transfers between devices, local(): lax.all_gather(w_up, 'dp', axis=1, tiled=True)  43.1 us
    all_to_all x1, blocking collectives, local(): lax.all_to_all(send_grad, 'expert', split_axis=0, concat_axis=0, tiled=True)  30.1 us
    all_to_all x1, blocking collectives, local(): lax.all_to_all(input_rows.reshape(expert_count, capacity, width), 'expert...  28.5 us
    all_to_all x1, waiting for transfers between devices, local(): lax.all_to_all(expert_out.reshape(expert_count, capacity, width), 'expert...  27.5 us
    unnamed x49, local copies, waits for them, and re-layouts  26 us
    all_to_all x1, waiting for transfers between devices, local(): lax.all_to_all(token_grad[None], 'dp', split_axis=2, concat_axis=1, tiled...  22.6 us
    unnamed x3, other arithmetic  19.7 us
  transfers between devices with their start and end apart: 12, of which 8 were waited for; matrix products, arithmetic and copies ran while one was open for 9% of the time, Pallas kernels for 0%

profile of v1, /device:TPU:0, one launch (start us, length us, event | category | flops | bytes accessed | tf_op | source)
XLA Modules:
  0.0 399.3 jit_solution(7506828545641787136)
XLA Ops:
  9.2 15.4 %collective-permute-done = bf16[1,128,3584]{2,1,0:T(8,128)(2,1)S(1)} collective-permute-done((bf16[1,128,3584]{2,1,0:T(8,128)(2,1)}, bf16[1,128,3584]{2,1,0:T(8,128)(2,1)S(1)}, u32[]{:S(2)}, u32[]{:S(2)}) %collective-permute-start) | collective-permute-done | bytes 917536 | tf_op jit(solution)/shard_map/ppermute | solution.py:13
  24.8 3.3 collective-permute-start.4
  28.1 38.9 %collective-permute-done.1 = bf16[1,128,3584]{2,1,0:T(8,128)(2,1)S(1)} collective-permute-done((bf16[1,128,3584]{2,1,0:T(8,128)(2,1)S(1)}, bf16[1,128,3584]{2,1,0:T(8,128)(2,1)S(1)}, u32[]{:S(2)}, u32[]{:S(2)}) %collective-permute-start.1) | collective-permute-done | bytes 917536 | tf_op jit(solution)/shard_map/ppermute | solution.py:13
  67.1 1.1 collective-permute-done.4
  68.2 3.6 collective-permute-start.5
  71.9 29.6 %collective-permute-done.2 = bf16[1,128,3584]{2,1,0:T(8,128)(2,1)} collective-permute-done((bf16[1,128,3584]{2,1,0:T(8,128)(2,1)S(1)}, bf16[1,128,3584]{2,1,0:T(8,128)(2,1)}, u32[]{:S(2)}, u32[]{:S(2)}) %collective-permute-start.2) | collective-permute-done | bytes 917536 | tf_op jit(solution)/shard_map/ppermute | solution.py:13
  101.4 6.0 %collective-permute-start.3 = (bf16[1,128,3584]{2,1,0:T(8,128)(2,1)}, bf16[1,128,3584]{2,1,0:T(8,128)(2,1)}, u32[]{:S(2)}, u32[]{:S(2)}) collective-permute-start(bf16[1,128,3584]{2,1,0:T(8,128)(2,1)} %collective-permute-done.2), channel_id=1, source_target_pairs={{0,4},{4,8},{8,12},{12,16},{16,20},{20,24},{24,28},{28,0},{1,5},{5... | collective-permute-start | bytes 2752520 | tf_op jit(solution)/shard_map/ppermute | solution.py:13
  108.4 1.3 concatenate.12
  110.9 3.7 gather_fusion
  114.6 4.6 %all-to-all-start = ((bf16[4,80,3584]{2,1,0:T(8,128)(2,1)}), bf16[4,80,3584]{2,1,0:T(8,128)(2,1)}, u32[]{:S(2)}, u32[]{:S(2)}) async-start(bf16[4,80,3584]{2,1,0:T(8,128)(2,1)} %bitcast.6), calls=%async_computation | async-start | bytes 4587520 | tf_op jit(solution)/shard_map/all_to_all | solution.py:48
  119.3 14.1 %collective-permute-done.3 = bf16[1,128,3584]{2,1,0:T(8,128)(2,1)} collective-permute-done((bf16[1,128,3584]{2,1,0:T(8,128)(2,1)}, bf16[1,128,3584]{2,1,0:T(8,128)(2,1)}, u32[]{:S(2)}, u32[]{:S(2)}) %collective-permute-start.3) | collective-permute-done | bytes 917536 | tf_op jit(solution)/shard_map/ppermute | solution.py:13
  133.4 2.2 constant_dynamic-update-slice_fusion.15
  135.6 2.2 constant_dynamic-update-slice_fusion.14
  137.8 1.0 constant_dynamic-update-slice_fusion.13
  139.8 1.0 constant_dynamic-update-slice_fusion.11
  140.8 1.0 constant_dynamic-update-slice_fusion.10
  141.8 2.2 constant_dynamic-update-slice_fusion.9
  144.0 1.0 constant_dynamic-update-slice_fusion.8
  145.0 2.2 constant_dynamic-update-slice_fusion.7
  147.2 2.3 constant_dynamic-update-slice_fusion.6
  149.5 1.0 constant_dynamic-update-slice_fusion.5
  151.4 1.0 constant_dynamic-update-slice_fusion.3
  152.4 1.0 constant_dynamic-update-slice_fusion.2
  153.4 2.2 constant_dynamic-update-slice_fusion.1
  155.6 1.0 constant_dynamic-update-slice_fusion
  156.6 6.3 %fusion.10 = f32[320,1024]{1,0:T(8,128)S(1)} fusion(bf16[320,3584]{1,0:T(8,128)(2,1)} %bitcast.7, bf16[1,3584,1024]{2,1,0:T(8,128)(2,1)} %all-gather.3.cloned.1.call-done), kind=kOutput, calls=%fused_computation.15 | convolution fusion | flops 2348810240 | bytes 10944512 | tf_op jit(solution)/shard_map/dot_general | solution.py:58
  163.0 43.1 %all-gather.5.cloned.1.call-done = bf16[1,3584,1024]{2,1,0:T(8,128)(2,1)} async-done(((bf16[1,448,1024]{2,1,0:T(8,128)(2,1)}), bf16[1,3584,1024]{2,1,0:T(8,128)(2,1)}) %all-gather.5.cloned.1.call-update) | async-done | bytes 7340048 | tf_op jit(solution)/shard_map/all_gather | solution.py:52
  206.0 6.3 %fusion.6 = f32[320,1024]{1,0:T(8,128)S(1)} fusion(bf16[320,3584]{1,0:T(8,128)(2,1)} %bitcast.7, bf16[1,3584,1024]{2,1,0:T(8,128)(2,1)} %all-gather.5.cloned.1.call-done), kind=kOutput, calls=%fused_computation.11 | convolution fusion | flops 2348810240 | bytes 10944512 | tf_op jit(solution)/shard_map/dot_general | solution.py:59
  212.3 7.5 %fusion.20 = bf16[320,3584]{1,0:T(8,128)(2,1)} fusion(bf16[1,2048,3584]{2,1,0:T(8,128)(2,1)} %constant_dynamic-update-slice_fusion, s32[]{:T(128)S(6)} %select_n.32, f32[320,1024]{1,0:T(8,128)S(1)} %fusion.6, f32[320,1024]{1,0:T(8,128)S(1)} %fusion.10), kind=kOutput, calls=%fused_computation.21 | convolution fusion | flops 2351923200 | bytes 12255236 | tf_op jit(solution)/shard_map/dot_general | solution.py:63
  219.9 4.8 %all-to-all-start.1 = ((bf16[4,80,3584]{2,1,0:T(8,128)(2,1)}), bf16[4,80,3584]{2,1,0:T(8,128)(2,1)S(1)}, u32[]{:S(2)}, u32[]{:S(2)}) async-start(bf16[4,80,3584]{2,1,0:T(8,128)(2,1)} %bitcast.71), calls=%async_computation.1 | async-start | bytes 4587520 | tf_op jit(solution)/shard_map/all_to_all | solution.py:66
  224.6 27.5 %all-to-all-done.1 = bf16[4,80,3584]{2,1,0:T(8,128)(2,1)S(1)} async-done(((bf16[4,80,3584]{2,1,0:T(8,128)(2,1)}), bf16[4,80,3584]{2,1,0:T(8,128)(2,1)S(1)}, u32[]{:S(2)}, u32[]{:S(2)}) %all-to-all-start.1) | async-done | bytes 2293792 | tf_op jit(solution)/shard_map/all_to_all | solution.py:66
  252.1 1.1 gather_fusion.1
  253.3 2.5 fusion.26
  255.8 3.1 gather_fusion.2
  258.9 30.1 %all_to_all.38 = bf16[4,80,3584]{2,1,0:T(8,128)(2,1)S(1)} all-to-all(bf16[4,80,3584]{2,1,0:T(8,128)(2,1)S(1)} %bitcast.66), channel_id=1, replica_groups=mesh['dp'=8,'expert'=4] {'expert'}, dimensions={0} | all-to-all | bytes 4587520 | tf_op jit(solution)/shard_map/all_to_all | solution.py:76
  289.0 5.8 %fusion = f32[320,1024]{1,0:T(8,128)S(1)} fusion(bf16[320,3584]{1,0:T(8,128)(2,1)S(1)} %bitcast.73, bf16[1,2048,3584]{2,1,0:T(8,128)(2,1)} %constant_dynamic-update-slice_fusion, s32[]{:T(128)S(6)} %select_n.32), kind=kOutput, calls=%fused_computation.5 | convolution fusion | flops 2348810240 | bytes 10944516 | tf_op jit(solution)/shard_map/dot_general | solution.py:78
  294.9 1.1 copy-done.10
  295.9 4.7 %fusion.4 = f32[320,3584]{1,0:T(8,128)} fusion(bf16[1,3584,1024]{2,1,0:T(8,128)(2,1)S(1)} %bitcast.84, f32[320,1024]{1,0:T(8,128)S(1)} %fusion, f32[320,1024]{1,0:T(8,128)S(1)} %copy-done.8), kind=kOutput, calls=%fused_computation.9 | convolution fusion | flops 2350776320 | bytes 14548992 | tf_op jit(solution)/shard_map/dot_general | solution.py:85
  300.7 6.0 %fusion.17 = bf16[320,3584]{1,0:T(8,128)(2,1)S(1)} fusion(f32[320,3584]{1,0:T(8,128)} %fusion.4, bf16[1,3584,1024]{2,1,0:T(8,128)(2,1)S(1)} %bitcast.82, f32[320,1024]{1,0:T(8,128)S(1)} %copy-done.8, f32[320,1024]{1,0:T(8,128)} %copy-done.10, f32[320,1024]{1,0:T(8,128)} %copy-done.9), kind=kOutput, calls=%fused_computation.20 | convolution fusion | flops 2354380800 | bytes 18153472 | tf_op jit(solution)/shard_map/dot_general | solution.py:83
  306.6 28.5 %all_to_all.39 = bf16[4,80,3584]{2,1,0:T(8,128)(2,1)S(1)} all-to-all(bf16[4,80,3584]{2,1,0:T(8,128)(2,1)S(1)} %bitcast.72), channel_id=1, replica_groups=mesh['dp'=8,'expert'=4] {'expert'}, dimensions={0} | all-to-all | bytes 4587520 | tf_op jit(solution)/shard_map/all_to_all | solution.py:87
  335.2 1.1 gather_fusion.3
  336.3 2.5 copy.14
  339.3 19.7 %reduce = bf16[3584,128]{1,0:T(8,128)(2,1)S(1)} reduce(bf16[3584,1,128]{2,1,0:T(2,128)(2,1)S(1)} %bitcast.67, bf16[]{:T(256)} %broadcast.104), dimensions={1}, to_apply=%bitcast.58.reduce_sub_computation | reduce | bytes 1835010
  359.0 1.2 reshape.155
  360.1 6.4 %all-to-all-start.4 = ((bf16[8,2,28672]{2,1,0:T(2,128)(2,1)}), bf16[8,2,28672]{2,1,0:T(2,128)(2,1)S(1)}, u32[]{:S(2)}, u32[]{:S(2)}) async-start(bf16[8,2,28672]{2,1,0:T(2,128)(2,1)} %reshape.155), calls=%async_computation.4 | async-start | bytes 1835008 | tf_op jit(solution)/shard_map/all_to_all | solution.py:95
  366.5 1.1 fusion.24
  367.6 22.6 %all-to-all-done.4 = bf16[8,2,28672]{2,1,0:T(2,128)(2,1)S(1)} async-done(((bf16[8,2,28672]{2,1,0:T(2,128)(2,1)}), bf16[8,2,28672]{2,1,0:T(2,128)(2,1)S(1)}, u32[]{:S(2)}, u32[]{:S(2)}) %all-to-all-start.4) | async-done | bytes 917536 | tf_op jit(solution)/shard_map/all_to_all | solution.py:95
  391.3 1.2 copy.19
  (58 shorter events, 8.0 us)
Async XLA Ops:
  7.2 102.5 %copy-start.5 = (s32[1,128]{1,0:T(1,128)S(1)}, s32[1,128]{1,0:T(1,128)}, u32[]{:S(2)}) copy-start(s32[1,128]{1,0:T(1,128)} %param.9) | copy-start | bytes 1540
  7.2 149.4 %all-gather.3.cloned.1.call-start = ((), (), s32[]{:S(2)}) async-start(), calls=%async_computation.5 | async-start | bytes 8257536 | tf_op jit(solution)/shard_map/all_gather | solution.py:51
  7.9 198.1 %all-gather.5.cloned.1.call-start = ((), (), s32[]{:S(2)}) async-start(), calls=%async_computation.6 | async-start | bytes 8257536 | tf_op jit(solution)/shard_map/all_gather | solution.py:52
  8.7 15.9 %collective-permute-start = (bf16[1,128,3584]{2,1,0:T(8,128)(2,1)}, bf16[1,128,3584]{2,1,0:T(8,128)(2,1)S(1)}, u32[]{:S(2)}, u32[]{:S(2)}) collective-permute-start(bf16[1,128,3584]{2,1,0:T(8,128)(2,1)} %param.13), channel_id=1, source_target_pairs={{0,4},{4,8},{8,12},{12,16},{16,20},{20,24},{24,28},{28,0},{1,5},{5... | collective-permute-start | bytes 2752520 | tf_op jit(solution)/shard_map/ppermute | solution.py:13
  24.6 42.5 %collective-permute-start.1 = (bf16[1,128,3584]{2,1,0:T(8,128)(2,1)S(1)}, bf16[1,128,3584]{2,1,0:T(8,128)(2,1)S(1)}, u32[]{:S(2)}, u32[]{:S(2)}) collective-permute-start(bf16[1,128,3584]{2,1,0:T(8,128)(2,1)S(1)} %collective-permute-done), channel_id=1, source_target_pairs={{0,4},{4,8},{8,12},{12,16},{16,20},{20,24},{24,28},{28,0},{1,5},{5... | collective-permute-start | bytes 2752520 | tf_op jit(solution)/shard_map/ppermute | solution.py:13
  24.8 43.4 %collective-permute-start.4 = (bf16[1,128,3584]{2,1,0:T(8,128)(2,1)}, bf16[1,128,3584]{2,1,0:T(8,128)(2,1)S(1)}, u32[]{:S(2)}, u32[]{:S(2)}) collective-permute-start(bf16[1,128,3584]{2,1,0:T(8,128)(2,1)} %param.13), channel_id=1, source_target_pairs={{0,28},{4,0},{8,4},{12,8},{16,12},{20,16},{24,20},{28,24},{1,29},{... | collective-permute-start | bytes 2752520 | tf_op jit(solution)/shard_map/ppermute | solution.py:15
  67.1 1.1 copy-start.3
  67.1 34.4 %collective-permute-start.2 = (bf16[1,128,3584]{2,1,0:T(8,128)(2,1)S(1)}, bf16[1,128,3584]{2,1,0:T(8,128)(2,1)}, u32[]{:S(2)}, u32[]{:S(2)}) collective-permute-start(bf16[1,128,3584]{2,1,0:T(8,128)(2,1)S(1)} %collective-permute-done.1), channel_id=1, source_target_pairs={{0,4},{4,8},{8,12},{12,16},{16,20},{20,24},{24,28},{28,0},{1,5},{5... | collective-permute-start | bytes 2752520 | tf_op jit(solution)/shard_map/ppermute | solution.py:13
  68.2 51.0 %collective-permute-start.5 = (bf16[1,128,3584]{2,1,0:T(8,128)(2,1)S(1)}, bf16[1,128,3584]{2,1,0:T(8,128)(2,1)}, u32[]{:S(2)}, u32[]{:S(2)}) collective-permute-start(bf16[1,128,3584]{2,1,0:T(8,128)(2,1)S(1)} %collective-permute-done.4), channel_id=1, source_target_pairs={{0,28},{4,0},{8,4},{12,8},{16,12},{20,16},{24,20},{28,24},{1,29},{... | collective-permute-start | bytes 2752520 | tf_op jit(solution)/shard_map/ppermute | solution.py:15
  101.4 32.0 %collective-permute-start.3 = (bf16[1,128,3584]{2,1,0:T(8,128)(2,1)}, bf16[1,128,3584]{2,1,0:T(8,128)(2,1)}, u32[]{:S(2)}, u32[]{:S(2)}) collective-permute-start(bf16[1,128,3584]{2,1,0:T(8,128)(2,1)} %collective-permute-done.2), channel_id=1, source_target_pairs={{0,4},{4,8},{8,12},{12,16},{16,20},{20,24},{24,28},{28,0},{1,5},{5... | collective-permute-start | bytes 2752520 | tf_op jit(solution)/shard_map/ppermute | solution.py:13
  114.6 42.1 %all-to-all-start = ((bf16[4,80,3584]{2,1,0:T(8,128)(2,1)}), bf16[4,80,3584]{2,1,0:T(8,128)(2,1)}, u32[]{:S(2)}, u32[]{:S(2)}) async-start(bf16[4,80,3584]{2,1,0:T(8,128)(2,1)} %bitcast.6), calls=%async_computation | async-start | bytes 4587520 | tf_op jit(solution)/shard_map/all_to_all | solution.py:48
  119.2 18.6 %copy-start.4 = (bf16[1,128,3584]{2,1,0:T(8,128)(2,1)S(1)}, bf16[1,128,3584]{2,1,0:T(8,128)(2,1)}, u32[]{:S(2)}) copy-start(bf16[1,128,3584]{2,1,0:T(8,128)(2,1)} %copy-done.3) | copy-start | bytes 2752516
  119.2 24.8 %collective-permute-start.6 = (bf16[1,128,3584]{2,1,0:T(8,128)(2,1)}, bf16[1,128,3584]{2,1,0:T(8,128)(2,1)S(1)}, u32[]{:S(2)}, u32[]{:S(2)}) collective-permute-start(bf16[1,128,3584]{2,1,0:T(8,128)(2,1)} %collective-permute-done.5), channel_id=1, source_target_pairs={{0,28},{4,0},{8,4},{12,8},{16,12},{20,16},{24,20},{28,24},{1,29},{... | collective-permute-start | bytes 2752520 | tf_op jit(solution)/shard_map/ppermute | solution.py:15
  137.8 2.0 copy-start.2
  162.9 49.4 %copy-start.7 = (f32[320,1024]{1,0:T(8,128)}, f32[320,1024]{1,0:T(8,128)S(1)}, u32[]{:S(2)}) copy-start(f32[320,1024]{1,0:T(8,128)S(1)} %fusion.10) | copy-start | bytes 3932164
  212.3 7.5 %copy-start.9 = (f32[320,1024]{1,0:T(8,128)}, f32[320,1024]{1,0:T(8,128)S(1)}, u32[]{:S(2)}) copy-start(f32[320,1024]{1,0:T(8,128)S(1)} %fusion.6) | copy-start | bytes 3932164
  219.9 32.2 %all-to-all-start.1 = ((bf16[4,80,3584]{2,1,0:T(8,128)(2,1)}), bf16[4,80,3584]{2,1,0:T(8,128)(2,1)S(1)}, u32[]{:S(2)}, u32[]{:S(2)}) async-start(bf16[4,80,3584]{2,1,0:T(8,128)(2,1)} %bitcast.71), calls=%async_computation.1 | async-start | bytes 4587520 | tf_op jit(solution)/shard_map/all_to_all | solution.py:66
  252.1 1.1 copy-start.6
  253.2 2.5 copy-start
  258.9 37.0 %slice-start.2 = ((s8[7340032]{0:T(1024)(128)(4,1)}), s8[4194304]{0:T(1024)(128)(4,1)S(1)}, s32[]{:S(2)}) async-start(s8[7340032]{0:T(1024)(128)(4,1)} %bitcast.83), calls=%async_computation.9 | async-start | bytes 8388608
  289.0 6.9 %slice-start.3 = ((s8[7340032]{0:T(1024)(128)(4,1)}), s8[3145728]{0:T(1024)(128)(4,1)S(1)}, s32[]{:S(2)}) async-start(s8[7340032]{0:T(1024)(128)(4,1)} %bitcast.83), calls=%async_computation.10 | async-start | bytes 6291456
  289.0 6.9 %copy-start.8 = (f32[320,1024]{1,0:T(8,128)S(1)}, f32[320,1024]{1,0:T(8,128)}, u32[]{:S(2)}) copy-start(f32[320,1024]{1,0:T(8,128)} %copy-done.7) | copy-start | bytes 3932164
  289.0 11.6 %slice-start = ((s8[7340032]{0:T(1024)(128)(4,1)}), s8[4194304]{0:T(1024)(128)(4,1)S(1)}, s32[]{:S(2)}) async-start(s8[7340032]{0:T(1024)(128)(4,1)} %bitcast.81), calls=%async_computation.7 | async-start | bytes 8388608
  294.8 1.1 copy-start.10
  295.9 4.7 %slice-start.1 = ((s8[7340032]{0:T(1024)(128)(4,1)}), s8[3145728]{0:T(1024)(128)(4,1)S(1)}, s32[]{:S(2)}) async-start(s8[7340032]{0:T(1024)(128)(4,1)} %bitcast.81), calls=%async_computation.8 | async-start | bytes 6291456
  359.0 7.5 %copy-start.1 = (bf16[128,3584]{1,0:T(8,128)(2,1)S(1)}, bf16[128,3584]{1,0:T(8,128)(2,1)}, u32[]{:S(2)}) copy-start(bf16[128,3584]{1,0:T(8,128)(2,1)} %copy-done) | copy-start | bytes 2752516
  360.1 30.1 %all-to-all-start.4 = ((bf16[8,2,28672]{2,1,0:T(2,128)(2,1)}), bf16[8,2,28672]{2,1,0:T(2,128)(2,1)S(1)}, u32[]{:S(2)}, u32[]{:S(2)}) async-start(bf16[8,2,28672]{2,1,0:T(2,128)(2,1)} %reshape.155), calls=%async_computation.4 | async-start | bytes 1835008 | tf_op jit(solution)/shard_map/all_to_all | solution.py:95
Sparse Core Ops, SparseCore 0:
  9.7 117.6 all-gather.2
  129.0 77.0 all-gather.4
